TPU v7x, 256 devices: a whole 4x4x8 slice. The times are simulated.
256 devices in a mesh: wide: 32 (over x_lo, z, core), narrow: 8 (over x_hi, y).
Axes of the slice: x: 4 (x_hi: 2, x_lo: 2; x = x_hi * 2 + x_lo), y: 4, z: 8, core: 2. Of those that a mesh axis runs over, the one named last changes fastest.
Arguments:
- activations: float32 [1024, 17408], P('wide', 'narrow'), may hold values from -6 to 6
- act_basis: float32 [17408, 17408], P('narrow', 'wide'), may hold values from -0.046875 to 0.046875
- grads: float32 [1024, 5120], P(None, 'wide'), may hold values from -0.3 to 0.3
- grad_basis: float32 [5120, 5120], P('wide', 'narrow'), may hold values from -0.078125 to 0.078125
- seq_ids: int32 [1024], replicated, may hold values from 0 to 3, never falling along the last dimension, each value on 1 to 512 neighbouring positions
Outputs:
- eigenvalues: float32 [17408, 5120], P('wide', 'narrow')
Inputs may be any that keep to these rules, and one draw needn't show every extreme that they name: `seq_ids`: never falling along the rows; every sequence has at least one row and at most 512 rows, and one sequence has exactly 512.
All inputs are finite; a program needn't handle non-finite values.
Results may differ from a plain program's by a relative error of at most 0.0003.
Values sent between devices are 32-bit elements; how exact they have to be, the bound alone decides.
No kernel may reach another device: no remote copies, remote signals or barrier semaphores. Data moves between devices by JAX's collectives and lax.ppermute only.
A program may use at most 64 MiB of HBM per device.

v0:
```python
import jax
import jax.numpy as jnp
from jax import lax
from jax.sharding import Mesh
from jax.sharding import PartitionSpec as P

SEQS = 4
SEQ_MOST = 512
WIDE = ("wide_0", "wide_1", "wide_2")


def filled_up(lines, devices):
    spare = -len(lines) % devices
    return jnp.pad(lines, [(0, spare)] + [(0, 0)] * (lines.ndim - 1))


def from_everyone(value, axis):
    devices = lax.axis_size(axis)
    return lax.all_to_all(
        jnp.broadcast_to(value[None], (devices, *value.shape)), axis, 0, 0, tiled=True
    )


def in_order(blocks, dim):
    blocks = jnp.moveaxis(blocks, 0, dim)
    dims = blocks.shape
    return blocks.reshape(*dims[:dim], dims[dim] * dims[dim + 1], *dims[dim + 2 :])


def gather_axes(value, axes, dim):
    far, near = axes
    first = from_everyone(value, far)
    blocks = jnp.swapaxes(from_everyone(first, near), 0, 1)
    return in_order(blocks.reshape(-1, *value.shape), dim)


def in_blocks(value, dim, devices):
    dims = value.shape
    blocks = value.reshape(*dims[:dim], devices, dims[dim] // devices, *dims[dim + 1 :])
    return jnp.moveaxis(blocks, dim, 0)


def sent_and_summed(value, axis, dim):
    blocks = in_blocks(value, dim, lax.axis_size(axis))
    arrived = lax.all_to_all(blocks, axis, split_axis=0, concat_axis=0, tiled=True)
    return arrived.sum(axis=0)


def summed_rows(value, axes, dim):
    far, near = axes
    blocks = in_blocks(value, dim, lax.axis_size(far))
    nearer = sent_and_summed(blocks, near, dim + 1)
    arrived = lax.all_to_all(nearer, far, split_axis=0, concat_axis=0, tiled=True)
    return arrived.sum(axis=0)


def nested_sum(value, axes):
    lines = value.reshape(-1, value.shape[-1])
    padded = filled_up(lines, lax.axis_size(axes[0]) * lax.axis_size(axes[1]))
    whole = gather_axes(summed_rows(padded, axes, 0), axes, 0)
    return lax.slice_in_dim(whole, 0, len(lines)).reshape(value.shape)


def seq_window(rotated_acts, rotated_grads, seq_ids, seq_label):
    token_rows = rotated_grads.shape[0]
    first_row = jnp.sum((seq_ids < seq_label).astype(jnp.int32))
    window_start = jnp.minimum(first_row, token_rows - SEQ_MOST)
    acts_window = lax.dynamic_slice_in_dim(rotated_acts, window_start, SEQ_MOST, 0)
    grads_window = lax.dynamic_slice_in_dim(rotated_grads, window_start, SEQ_MOST, 0)
    ids_window = lax.dynamic_slice_in_dim(seq_ids, window_start, SEQ_MOST, 0)
    seq_mask = (ids_window == seq_label).astype(jnp.float32)[:, None]
    return (acts_window, grads_window * seq_mask)


def per_device(activations, act_basis, grads, grad_basis, seq_ids):
    highest = lax.Precision.HIGHEST
    gathered = lax.all_gather(activations, WIDE, axis=0, tiled=True)
    partial_acts = jnp.dot(
        gathered, act_basis, precision=highest, preferred_element_type=jnp.float32
    )
    rotated_acts = lax.psum(partial_acts, "narrow")
    partial_grads = jnp.dot(
        grads, grad_basis, precision=highest, preferred_element_type=jnp.float32
    )
    rotated_grads = nested_sum(partial_grads, (("wide_0", "wide_1"), "wide_2"))
    out_cols = rotated_grads.shape[1]
    running = jnp.zeros((rotated_acts.shape[1], out_cols), jnp.float32)
    for seq_label in range(SEQS):
        acts_window, grads_window = seq_window(rotated_acts, rotated_grads, seq_ids, seq_label)
        moment = jnp.dot(
            acts_window.T, grads_window, precision=highest, preferred_element_type=jnp.float32
        )
        running = running + moment * moment
    return running / jnp.float32(SEQS)


def solution(mesh):
    split = Mesh(
        mesh.devices.reshape(2, 8, 2, mesh.shape["narrow"]),
        ("wide_0", "wide_1", "wide_2", "narrow"),
    )
    return jax.shard_map(
        per_device,
        mesh=split,
        in_specs=(P(WIDE, "narrow"), P("narrow", WIDE), P(None, WIDE), P(WIDE, "narrow"), P()),
        out_specs=P(WIDE, "narrow"),
        check_vma=False,
    )
```

profile of v0, /device:TPU:32, one launch (start us, length us, event | category | flops | bytes accessed | tf_op | source)
XLA Modules:
  0.0 276.0 jit_solution(7294936986308628746)
XLA Ops:
  6.5 0.0 copy-start
  6.5 0.0 all-gather.2.cloned.1.call-start
  6.5 0.7 all-gather.2.cloned.1.call-update
  7.3 0.4 copy-done
  7.6 3.9 %fusion.29 = f32[1024,640]{1,0:T(8,128)S(1)} fusion(f32[1024,160]{0,1:T(8,128)S(1)} %copy-done, f32[160,640]{1,0:T(8,128)} %param.8), kind=kOutput, calls=%fused_computation.42 | convolution fusion | flops 1258291200 | bytes 3686400 | tf_op jit(solution)/shard_map/dot_general | solution.py:82
  11.6 0.2 copy.11
  11.8 5.8 %all_to_all.20 = f32[2,16,32,640]{3,2,1,0:T(8,128)S(1)} all-to-all(f32[2,16,32,640]{3,2,1,0:T(8,128)S(1)} %bitcast.15), channel_id=1, replica_groups=mesh['wide_0'=2,'wide_1'=8,'wide_2'=2,'narrow'=8] {'wide_2'}, dimensions={0} | all-to-all | bytes 5242880 | tf_op jit(solution)/shard_map/all_to_all | solution.py:45
  17.6 1.3 reduce_sum.55
  18.9 54.5 %all_to_all.21 = f32[16,32,640]{2,1,0:T(8,128)S(1)} all-to-all(f32[16,32,640]{2,1,0:T(8,128)} %reduce_sum.55), channel_id=1, replica_groups=mesh['wide_0'=2,'wide_1'=8,'wide_2'=2,'narrow'=8] {'wide_0','wide_1'}, dimensions={0} | all-to-all | bytes 2621440 | tf_op jit(solution)/shard_map/all_to_all | solution.py:53
  73.5 0.1 reduce_sum.56
  73.5 1.2 broadcast_in_dim.4
  74.7 6.4 %all-to-all-start.2 = ((f32[16,32,640]{2,1,0:T(8,128)}), f32[16,32,640]{2,1,0:T(8,128)S(1)}, u32[]{:S(2)}, u32[]{:S(2)}) async-start(f32[16,32,640]{2,1,0:T(8,128)} %broadcast_in_dim.4), calls=%async_computation.2 | async-start | bytes 2621440 | tf_op jit(solution)/shard_map/all_to_all | solution.py:19
  81.2 0.0 all-reduce.2.cloned.1.call-start
  81.2 52.6 %all-gather.2.cloned.1.call-done = f32[1024,2176]{1,0:T(8,128)} async-done(((f32[32,2176]{1,0:T(8,128)}), f32[1024,2176]{1,0:T(8,128)}) %all-gather.2.cloned.1.call-update) | async-done | bytes 8912912 | tf_op jit(solution)/shard_map/all_gather | solution.py:77
  133.8 21.9 %fusion.28 = f32[1024,544]{0,1:T(8,128)} fusion(f32[1024,2176]{1,0:T(8,128)} %all-gather.2.cloned.1.call-done, f32[2176,544]{0,1:T(8,128)} %param.6), kind=kOutput, calls=%fused_computation.41 | convolution fusion | flops 14545846272 | bytes 15876096 | tf_op jit(solution)/shard_map/dot_general | solution.py:78
  155.7 0.0 copy-start.2
  155.7 0.0 all-reduce.2.cloned.1.call-update
  155.7 0.7 copy-done.2
  156.4 0.7 convert_reduce_fusion
  159.8 0.1 fusion.27
  159.9 0.0 all-to-all-done.2
  159.9 0.3 broadcast_in_dim.5
  160.2 5.8 %all_to_all.22 = f32[2,16,32,640]{3,2,1,0:T(8,128)S(1)} all-to-all(f32[2,16,32,640]{3,2,1,0:T(8,128)S(1)} %broadcast_in_dim.5), channel_id=1, replica_groups=mesh['wide_0'=2,'wide_1'=8,'wide_2'=2,'narrow'=8] {'wide_2'}, dimensions={0} | all-to-all | bytes 5242880 | tf_op jit(solution)/shard_map/all_to_all | solution.py:19
  166.0 0.2 copy.9
  166.2 87.8 %all-reduce.2.cloned.1.call-done = f32[1024,544]{0,1:T(8,128)} async-done(((f32[1024,544]{0,1:T(8,128)}), f32[1024,544]{0,1:T(8,128)}) %all-reduce.2.cloned.1.call-update) | async-done | bytes 2228240 | tf_op jit(solution)/shard_map/psum | solution.py:81
  254.0 0.0 copy-start.1
  254.0 4.5 %convolution_multiply_fusion.1 = f32[544,640]{1,0:T(8,128)S(1)} fusion(f32[1024,640]{1,0:T(8,128)S(1)} %bitcast.11, s32[]{:T(128)S(6)} %select_n.10, f32[1024,544]{0,1:T(8,128)} %all-reduce.2.cloned.1.call-done, f32[512]{0:T(512)S(1)} %get-tuple-element.10), kind=kOutput, calls=%fused_computation.2 | convolution fusion | flops 2139770880 | bytes 3820544 | tf_op jit(solution)/shard_map/dot_general | solution.py:90
  258.5 0.0 copy-done.1
  258.5 3.1 %convolution_multiply_fusion.2 = f32[544,640]{1,0:T(8,128)S(1)} fusion(f32[1024,640]{1,0:T(8,128)S(1)} %bitcast.12, s32[]{:T(128)S(6)} %select_n.9, f32[1024,544]{0,1:T(8,128)S(1)} %copy-done.1, f32[512]{0:T(512)S(1)} %get-tuple-element.12), kind=kOutput, calls=%fused_computation.3 | convolution fusion | flops 2139770880 | bytes 3820544 | tf_op jit(solution)/shard_map/dot_general | solution.py:90
  261.7 3.2 %fusion.1 = f32[544,640]{1,0:T(8,128)S(1)} fusion(f32[544,640]{1,0:T(8,128)S(1)} %convolution_multiply_fusion.1, f32[544,640]{1,0:T(8,128)S(1)} %convolution_multiply_fusion.2, f32[1024,640]{1,0:T(8,128)S(1)} %bitcast.13, s32[]{:T(128)S(6)} %select_n.8, f32[1024,544]{0,1:T(8,128)S(1)} %copy-done.1, f32[512]{0:T(512)S(1)} %get-tuple-element.11), kind=kOutput, calls=%fused_computation.6 | convolution fusion | flops 2140467200 | bytes 6605824 | tf_op jit(solution)/shard_map/dot_general | solution.py:90
  264.9 4.2 %fusion.3 = f32[544,640]{1,0:T(8,128)} fusion(f32[544,640]{1,0:T(8,128)S(1)} %fusion.1, f32[1024,640]{1,0:T(8,128)S(1)} %bitcast.14, s32[]{:T(128)S(6)} %select_n.11, f32[1024,544]{0,1:T(8,128)S(1)} %copy-done.1, f32[512]{0:T(512)S(1)} %get-tuple-element.9), kind=kOutput, calls=%fused_computation.8 | convolution fusion | flops 2140467200 | bytes 5213184 | tf_op jit(solution)/shard_map/dot_general | solution.py:90
Async XLA Ops:
  6.5 1.1 copy-start
  6.5 127.2 %all-gather.2.cloned.1.call-start = ((), (), s32[]{:S(2)}) async-start(), calls=%async_computation.4 | async-start | bytes 9191424 | tf_op jit(solution)/shard_map/all_gather | solution.py:77
  74.7 85.1 %all-to-all-start.2 = ((f32[16,32,640]{2,1,0:T(8,128)}), f32[16,32,640]{2,1,0:T(8,128)S(1)}, u32[]{:S(2)}, u32[]{:S(2)}) async-start(f32[16,32,640]{2,1,0:T(8,128)} %broadcast_in_dim.4), calls=%async_computation.2 | async-start | bytes 2621440 | tf_op jit(solution)/shard_map/all_to_all | solution.py:19
  81.2 172.9 %all-reduce.2.cloned.1.call-start = ((), (), s32[]{:S(2)}) async-start(), calls=%async_computation.5 | async-start | bytes 4456448 | tf_op jit(solution)/shard_map/psum | solution.py:81
  155.7 0.7 copy-start.2
  254.0 4.5 %copy-start.1 = (f32[1024,544]{0,1:T(8,128)S(1)}, f32[1024,544]{0,1:T(8,128)}, u32[]{:S(2)}) copy-start(f32[1024,544]{0,1:T(8,128)} %all-reduce.2.cloned.1.call-done) | copy-start | bytes 6684676
Sparse Core Ops, SparseCore 0:
  9.2 124.5 all-gather.1
  155.9 98.0 all-reduce.1
where the time goes:
time: 276 us
  waiting for transfers between devices  141 us (51%)
  blocking collectives  66.2 us (24%)
  matrix products  41 us (15%)
  between operations  16.1 us (6%)
  starting transfers between devices  6.48 us (2%)
  local copies, waits for them, and re-layouts  2.9 us (1%)
    psum x1, waiting for transfers between devices, per_device(): rotated_acts = lax.psum(partial_acts, 'narrow')  87.8 us
    all_to_all x1, blocking collectives, summed_rows(): lax.all_to_all(nearer, far, split_axis=0, concat_axis=0, tiled=True)  54.5 us
    all_gather x1, waiting for transfers between devices, per_device(): gathered = lax.all_gather(activations, WIDE, axis=0, tiled=True)  52.6 us
    dot_general x1, matrix products, per_device(): jnp.dot(gathered, act_basis, precision=highest, preferred_element_type=jn...  21.9 us
    dot_general x4, matrix products, per_device(): jnp.dot(acts_window.T, grads_window, precision=highest, preferred_element...  15.1 us
    all_to_all x1, starting transfers between devices, from_everyone(): lax.all_to_all(jnp.broadcast_to(value[None], (devices, *value.shape)), ax...  6.44 us
    all_to_all x1, blocking collectives, from_everyone(): lax.all_to_all(jnp.broadcast_to(value[None], (devices, *value.shape)), ax...  5.84 us
    all_to_all x1, blocking collectives, sent_and_summed(): lax.all_to_all(blocks, axis, split_axis=0, concat_axis=0, tiled=True)  5.84 us
  transfers between devices with their start and end apart: 3, of which 2 were waited for; matrix products, arithmetic and copies ran while one was open for 11% of the time, Pallas kernels for 0%

commit v1 on v0

--- a/solution.py
+++ b/solution.py
@@ -74,7 +74,9 @@
 
 def per_device(activations, act_basis, grads, grad_basis, seq_ids):
     highest = lax.Precision.HIGHEST
-    gathered = lax.all_gather(activations, WIDE, axis=0, tiled=True)
+    gathered = jnp.concatenate(
+        lax.all_to_all(jnp.stack([activations] * lax.axis_size(WIDE)), WIDE, 0, 0), axis=0
+    )
     partial_acts = jnp.dot(
         gathered, act_basis, precision=highest, preferred_element_type=jnp.float32
     )

time: 276 us -> 421 us (1.53)
  waiting for transfers between devices: 141 us -> 283 us
  blocking collectives: 66.2 us -> 54.4 us
  starting transfers between devices: 6.48 us -> 16.2 us
  local copies, waits for them, and re-layouts: 2.9 us -> 8.1 us
    all_to_all x0 -> x1, waiting for transfers between devices: none -> 194 us  [per_device(): lax.all_to_all(jnp.stack([activations] * lax.axis_size(WIDE)), WIDE, 0, 0)]
    all_gather x1 -> x0, waiting for transfers between devices: 52.6 us -> none  [per_device(): gathered = lax.all_gather(activations, WIDE, axis=0, tiled=True)]
    all_to_all x1, blocking collectives: 54.5 us -> 42.7 us  [summed_rows(): lax.all_to_all(nearer, far, split_axis=0, concat_axis=0, tiled=True)]
    all_to_all x1, waiting for transfers between devices: 0.01 us -> 5.62 us  [from_everyone(): lax.all_to_all(jnp.broadcast_to(value[None], (devices, *value.shape)), ax...]
    all_to_all x1, starting transfers between devices: 6.44 us -> 11.4 us  [from_everyone(): lax.all_to_all(jnp.broadcast_to(value[None], (devices, *value.shape)), ax...]
    all_to_all x0 -> x1, starting transfers between devices: none -> 4.75 us  [per_device(): lax.all_to_all(jnp.stack([activations] * lax.axis_size(WIDE)), WIDE, 0, 0)]
    another operation x0 -> x1, local copies, waits for them, and re-layouts: none -> 4.47 us  [per_device(): jnp.stack([activations] * lax.axis_size(WIDE))]
    psum x1, waiting for transfers between devices: 87.8 us -> 83.3 us  [per_device(): rotated_acts = lax.psum(partial_acts, 'narrow')]
  transfers between devices with their start and end apart: 3 -> 3, of which waited for: 2 -> 3; matrix products, arithmetic and copies ran while one was open for 11% -> 6% of each run, Pallas kernels for 0% -> 0%
where the time goes in v1:
time: 421 us
  waiting for transfers between devices  283 us (67%)
  blocking collectives  54.4 us (13%)
  matrix products  41 us (10%)
  starting transfers between devices  16.2 us (4%)
  between operations  16.1 us (4%)
  local copies, waits for them, and re-layouts  8.1 us (2%)
    all_to_all x1, waiting for transfers between devices, per_device(): lax.all_to_all(jnp.stack([activations] * lax.axis_size(WIDE)), WIDE, 0, 0)  194 us
    psum x1, waiting for transfers between devices, per_device(): rotated_acts = lax.psum(partial_acts, 'narrow')  83.3 us
    all_to_all x1, blocking collectives, summed_rows(): lax.all_to_all(nearer, far, split_axis=0, concat_axis=0, tiled=True)  42.7 us
    dot_general x1, matrix products, per_device(): jnp.dot(gathered, act_basis, precision=highest, preferred_element_type=jn...  21.9 us
    dot_general x4, matrix products, per_device(): jnp.dot(acts_window.T, grads_window, precision=highest, preferred_element...  15.1 us
    all_to_all x1, starting transfers between devices, from_everyone(): lax.all_to_all(jnp.broadcast_to(value[None], (devices, *value.shape)), ax...  11.4 us
  transfers between devices with their start and end apart: 3, of which 3 were waited for; matrix products, arithmetic and copies ran while one was open for 6% of the time, Pallas kernels for 0%

profile of v1, /device:TPU:32, one launch (start us, length us, event | category | flops | bytes accessed | tf_op | source)
XLA Modules:
  0.0 420.9 jit_solution(15228253331422481288)
XLA Ops:
  6.5 0.0 copy-start
  6.5 1.1 copy-done
  7.6 3.9 fusion.29
  11.6 0.2 copy.11
  11.8 5.8 %all_to_all.25 = f32[2,16,32,640]{3,2,1,0:T(8,128)S(1)} all-to-all(f32[2,16,32,640]{3,2,1,0:T(8,128)S(1)} %bitcast.16), channel_id=1, replica_groups=mesh['wide_0'=2,'wide_1'=8,'wide_2'=2,'narrow'=8] {'wide_2'}, dimensions={0} | all-to-all | bytes 5242880 | tf_op jit(solution)/shard_map/all_to_all | solution.py:45
  17.6 1.3 reduce_sum.55
  18.9 0.0 copy-start.2
  18.9 42.7 %all_to_all.26 = f32[16,32,640]{2,1,0:T(8,128)S(1)} all-to-all(f32[16,32,640]{2,1,0:T(8,128)} %reduce_sum.55), channel_id=1, replica_groups=mesh['wide_0'=2,'wide_1'=8,'wide_2'=2,'narrow'=8] {'wide_0','wide_1'}, dimensions={0} | all-to-all | bytes 2621440 | tf_op jit(solution)/shard_map/all_to_all | solution.py:53
  61.7 0.0 copy-done.2
  61.7 4.5 %stack.2 = f32[32,32,2176]{2,1,0:T(8,128)} broadcast(f32[32,2176]{1,0:T(8,128)S(1)} %copy-done.2), dimensions={1,2} | broadcast | bytes 9191424 | tf_op jit(solution)/shard_map/stack | solution.py:78
  66.1 4.8 %all-to-all-start = ((f32[32,32,2176]{2,1,0:T(8,128)}), f32[32,32,2176]{2,1,0:T(8,128)}, u32[]{:S(2)}, u32[]{:S(2)}) async-start(f32[32,32,2176]{2,1,0:T(8,128)} %stack.2), calls=%async_computation | async-start | bytes 17825792 | tf_op jit(solution)/shard_map/all_to_all | solution.py:78
  70.9 0.1 reduce_sum.56
  71.0 194.0 %all-to-all-done = f32[32,32,2176]{2,1,0:T(8,128)} async-done(((f32[32,32,2176]{2,1,0:T(8,128)}), f32[32,32,2176]{2,1,0:T(8,128)}, u32[]{:S(2)}, u32[]{:S(2)}) %all-to-all-start) | async-done | bytes 8912928 | tf_op jit(solution)/shard_map/all_to_all | solution.py:78
  264.9 1.2 broadcast_in_dim.4
  266.1 11.4 %all-to-all-start.3 = ((f32[16,32,640]{2,1,0:T(8,128)}), f32[16,32,640]{2,1,0:T(8,128)S(1)}, u32[]{:S(2)}, u32[]{:S(2)}) async-start(f32[16,32,640]{2,1,0:T(8,128)} %broadcast_in_dim.4), calls=%async_computation.3 | async-start | bytes 2621440 | tf_op jit(solution)/shard_map/all_to_all | solution.py:19
  277.5 0.0 all-reduce.2.cloned.1.call-start
  277.5 21.9 %fusion.28 = f32[1024,544]{0,1:T(8,128)} fusion(f32[1024,2176]{1,0:T(8,128)} %bitcast, f32[2176,544]{0,1:T(8,128)} %param.6), kind=kOutput, calls=%fused_computation.41 | convolution fusion | flops 14545846272 | bytes 15876096 | tf_op jit(solution)/shard_map/dot_general | solution.py:80
  299.5 0.0 copy-start.3
  299.5 0.0 all-reduce.2.cloned.1.call-update
  299.5 0.7 copy-done.3
  300.2 0.7 convert_reduce_fusion
  303.5 0.1 fusion.27
  303.6 5.6 %all-to-all-done.3 = f32[16,32,640]{2,1,0:T(8,128)S(1)} async-done(((f32[16,32,640]{2,1,0:T(8,128)}), f32[16,32,640]{2,1,0:T(8,128)S(1)}, u32[]{:S(2)}, u32[]{:S(2)}) %all-to-all-start.3) | async-done | bytes 1310752 | tf_op jit(solution)/shard_map/all_to_all | solution.py:19
  309.2 0.3 broadcast_in_dim.5
  309.5 5.8 %all_to_all.27 = f32[2,16,32,640]{3,2,1,0:T(8,128)S(1)} all-to-all(f32[2,16,32,640]{3,2,1,0:T(8,128)S(1)} %broadcast_in_dim.5), channel_id=1, replica_groups=mesh['wide_0'=2,'wide_1'=8,'wide_2'=2,'narrow'=8] {'wide_2'}, dimensions={0} | all-to-all | bytes 5242880 | tf_op jit(solution)/shard_map/all_to_all | solution.py:19
  315.4 0.2 copy.9
  315.6 83.3 %all-reduce.2.cloned.1.call-done = f32[1024,544]{0,1:T(8,128)} async-done(((f32[1024,544]{0,1:T(8,128)}), f32[1024,544]{0,1:T(8,128)}) %all-reduce.2.cloned.1.call-update) | async-done | bytes 2228240 | tf_op jit(solution)/shard_map/psum | solution.py:83
  398.9 0.0 copy-start.1
  398.9 4.5 %convolution_multiply_fusion.1 = f32[544,640]{1,0:T(8,128)S(1)} fusion(f32[1024,640]{1,0:T(8,128)S(1)} %bitcast.12, s32[]{:T(128)S(6)} %select_n.10, f32[1024,544]{0,1:T(8,128)} %all-reduce.2.cloned.1.call-done, f32[512]{0:T(512)S(1)} %get-tuple-element.10), kind=kOutput, calls=%fused_computation.2 | convolution fusion | flops 2139770880 | bytes 3820544 | tf_op jit(solution)/shard_map/dot_general | solution.py:92
  403.4 0.0 copy-done.1
  403.4 3.1 convolution_multiply_fusion.2
  406.6 3.2 fusion.1
  409.8 4.2 %fusion.3 = f32[544,640]{1,0:T(8,128)} fusion(f32[544,640]{1,0:T(8,128)S(1)} %fusion.1, f32[1024,640]{1,0:T(8,128)S(1)} %bitcast.15, s32[]{:T(128)S(6)} %select_n.11, f32[1024,544]{0,1:T(8,128)S(1)} %copy-done.1, f32[512]{0:T(512)S(1)} %get-tuple-element.9), kind=kOutput, calls=%fused_computation.8 | convolution fusion | flops 2140467200 | bytes 5213184 | tf_op jit(solution)/shard_map/dot_general | solution.py:92
Async XLA Ops:
  6.5 1.1 copy-start
  18.9 42.7 %copy-start.2 = (f32[32,2176]{1,0:T(8,128)S(1)}, f32[32,2176]{1,0:T(8,128)}, u32[]{:S(2)}) copy-start(f32[32,2176]{1,0:T(8,128)} %param.5) | copy-start | bytes 835588
  66.1 198.8 %all-to-all-start = ((f32[32,32,2176]{2,1,0:T(8,128)}), f32[32,32,2176]{2,1,0:T(8,128)}, u32[]{:S(2)}, u32[]{:S(2)}) async-start(f32[32,32,2176]{2,1,0:T(8,128)} %stack.2), calls=%async_computation | async-start | bytes 17825792 | tf_op jit(solution)/shard_map/all_to_all | solution.py:78
  266.1 43.1 %all-to-all-start.3 = ((f32[16,32,640]{2,1,0:T(8,128)}), f32[16,32,640]{2,1,0:T(8,128)S(1)}, u32[]{:S(2)}, u32[]{:S(2)}) async-start(f32[16,32,640]{2,1,0:T(8,128)} %broadcast_in_dim.4), calls=%async_computation.3 | async-start | bytes 2621440 | tf_op jit(solution)/shard_map/all_to_all | solution.py:19
  277.5 121.4 %all-reduce.2.cloned.1.call-start = ((), (), s32[]{:S(2)}) async-start(), calls=%async_computation.5 | async-start | bytes 4456448 | tf_op jit(solution)/shard_map/psum | solution.py:83
  299.5 0.7 copy-start.3
  398.9 4.5 %copy-start.1 = (f32[1024,544]{0,1:T(8,128)S(1)}, f32[1024,544]{0,1:T(8,128)}, u32[]{:S(2)}) copy-start(f32[1024,544]{0,1:T(8,128)} %all-reduce.2.cloned.1.call-done) | copy-start | bytes 6684676
Sparse Core Ops, SparseCore 0:
  299.6 99.2 all-reduce.1
